TPU v7x, 32 devices: a whole 2x2x4 slice. The times are simulated.
32 devices in a mesh: dp: 4 (over z), seq: 8 (over y, x, core).
Axes of the slice: x: 2, y: 2, z: 4, core: 2. Of those that a mesh axis runs over, the one named last changes fastest.
Arguments:
- tokens: bfloat16 [1024, 2880], P('seq', 'dp'), may hold values from -6 to 6
- upstream: bfloat16 [1024, 2880], P('seq', 'dp'), may hold values from -6 to 6
- norm_gain: bfloat16 [2880], replicated, may hold values from 0.5 to 1.5
- experts: int32 [1024, 4], P('seq'), may hold values from 0 to 15, all different within a row; in each aligned block of 128 rows (0 to 127, 128 to 255, ...) at most 48 rows name the same one
- route_weights: bfloat16 [1024, 4], P('seq'), may hold values from 0.049804688 to 0.59765625
- w_gate_up: bfloat16 [16, 2880, 2, 1440], P('seq', None, None, 'dp'), may hold values from -0.109375 to 0.109375
- w_down: bfloat16 [16, 1440, 2880], P('seq', 'dp'), may hold values from -0.15625 to 0.15625
Outputs:
- token_gradient: bfloat16 [1024, 2880], P('seq', 'dp')
- gain_gradient: float32 [2880], P('dp')
- grad_weights: float32 [1024, 4], P('seq')
- grad_gate_up: bfloat16 [16, 2880, 2, 1440], P('seq', None, None, 'dp')
- grad_down: bfloat16 [16, 1440, 2880], P('seq', 'dp')
Inputs may be any that keep to these rules, and one draw needn't show every extreme that they name: Each row names 4 different experts. In each aligned block of 128 rows (the tokens of one index of seq) no expert is named more than 48 times, a bound that some block reaches.
All inputs are finite; a program needn't handle non-finite values.
Results may differ from a plain program's by a relative error of at most 0.012.
Values may be sent and summed in bfloat16 or wider, within the bound.
A program may use at most 128 MiB of HBM per device.

v0:
```python
import jax
import jax.numpy as jnp
from jax import lax
from jax.sharding import PartitionSpec as P


def expert_terms(x_rows, dy_rows, weight_rows, w_gu, w_dn):
    width = x_rows.shape[1]
    hidden = w_dn.shape[0]
    flat_gu = w_gu.reshape(width, 2 * hidden)
    projected = jnp.dot(x_rows, flat_gu, preferred_element_type=jnp.float32)
    gate_pre = projected[:, :hidden]
    up_pre = projected[:, hidden:]
    sig_gate = jax.nn.sigmoid(1.702 * gate_pre)
    glu_value = gate_pre * sig_gate
    activated = ((up_pre + 1.0) * glu_value).astype(jnp.bfloat16)
    back_proj = lax.dot_general(
        dy_rows, w_dn, (((1,), (1,)), ((), ())), preferred_element_type=jnp.float32
    )
    row_weight = weight_rows.astype(jnp.float32)[:, None]
    weight_grad = jnp.sum(activated.astype(jnp.float32) * back_proj, axis=1)
    dact = row_weight * back_proj
    dgate_pre = dact * (up_pre + 1.0) * (sig_gate + 1.702 * gate_pre * sig_gate * (1.0 - sig_gate))
    dup_pre = dact * glu_value
    dproj = jnp.concatenate([dgate_pre, dup_pre], axis=1).astype(jnp.bfloat16)
    scaled = (row_weight * activated.astype(jnp.float32)).astype(jnp.bfloat16)
    grad_dn = lax.dot_general(
        scaled, dy_rows, (((0,), (0,)), ((), ())), preferred_element_type=jnp.float32
    )
    grad_gu = lax.dot_general(
        x_rows, dproj, (((0,), (0,)), ((), ())), preferred_element_type=jnp.float32
    )
    grad_rows = lax.dot_general(
        dproj, flat_gu, (((1,), (1,)), ((), ())), preferred_element_type=jnp.float32
    )
    return (grad_gu, grad_dn, grad_rows, weight_grad)


def body(tokens, upstream, norm_gain, experts, route_weights, w_gate_up, w_down):
    dp_count = lax.axis_size("dp")
    seq_count = lax.axis_size("seq")
    token_row_list, part_width = tokens.shape
    width = part_width * dp_count
    picked_count = experts.shape[1]
    exp_local = w_gate_up.shape[0]
    hidden = w_down.shape[1]
    exp_total = exp_local * seq_count
    capacity = token_row_list * picked_count * 3 // (2 * exp_total)
    slot_total = exp_total * capacity
    gain_single = norm_gain.astype(jnp.float32)
    gain_part = lax.dynamic_slice_in_dim(
        gain_single, lax.axis_index("dp") * part_width, part_width, 0
    )
    token_piece = tokens.astype(jnp.float32)
    pair_experts = experts.reshape(-1)
    onehot = (pair_experts[:, None] == jnp.arange(exp_total, dtype=jnp.int32)[None, :]).astype(
        jnp.int32
    )
    rank = jnp.sum((jnp.cumsum(onehot, axis=0) - 1) * onehot, axis=1)
    position = pair_experts * capacity + rank
    placing = (position[None, :] == jnp.arange(slot_total, dtype=jnp.int32)[:, None]).astype(
        jnp.bfloat16
    )
    mover = jnp.sum(placing.reshape(slot_total, token_row_list, picked_count), axis=2)
    slot_weights = jnp.dot(
        placing, route_weights.reshape(-1), preferred_element_type=jnp.float32
    ).astype(jnp.bfloat16)
    full_tok, full_dy = (
        lax.all_gather(tokens, "dp", axis=1, tiled=True),
        lax.all_gather(upstream, "dp", axis=1, tiled=True),
    )
    full_f32 = full_tok.astype(jnp.float32)
    reciprocal_root_mean = lax.rsqrt(jnp.mean(full_f32 * full_f32, axis=1) + 1e-05)
    normalized_rows = (full_f32 * reciprocal_root_mean[:, None] * gain_single[None, :]).astype(
        jnp.bfloat16
    )
    send_tok = jnp.dot(mover, normalized_rows, preferred_element_type=jnp.float32).astype(
        jnp.bfloat16
    )
    send_dy = jnp.dot(mover, full_dy, preferred_element_type=jnp.float32).astype(jnp.bfloat16)
    feat_width = send_tok.shape[1]
    got_tok, got_dy, got_weight = (
        lax.all_to_all(
            send_tok.reshape(exp_total, capacity, feat_width),
            "seq",
            split_axis=0,
            concat_axis=0,
            tiled=True,
        ),
        lax.all_to_all(
            send_dy.reshape(exp_total, capacity, feat_width),
            "seq",
            split_axis=0,
            concat_axis=0,
            tiled=True,
        ),
        lax.all_to_all(
            slot_weights.reshape(exp_total, capacity),
            "seq",
            split_axis=0,
            concat_axis=0,
            tiled=True,
        ),
    )
    got_tok = got_tok.reshape(seq_count, exp_local, capacity, feat_width)
    got_dy = got_dy.reshape(seq_count, exp_local, capacity, feat_width)
    got_weight = got_weight.reshape(seq_count, exp_local, capacity)
    grads_gu = []
    grads_dn = []
    rows_list = []
    weight_list = []
    for member in range(exp_local):
        x_rows = got_tok[:, member].reshape(seq_count * capacity, width)
        dy_rows = got_dy[:, member].reshape(seq_count * capacity, width)
        weight_rows = got_weight[:, member].reshape(seq_count * capacity)
        results = expert_terms(x_rows, dy_rows, weight_rows, w_gate_up[member], w_down[member])
        grads_gu.append(results[0].reshape(width, 2, hidden).astype(jnp.bfloat16))
        grads_dn.append(results[1].astype(jnp.bfloat16))
        rows_list.append(results[2].reshape(seq_count, capacity, width))
        weight_list.append(results[3].reshape(seq_count, capacity))
    rows_stack = jnp.stack(rows_list, axis=1).reshape(exp_total, capacity, width)
    weight_stack = jnp.stack(weight_list, axis=1).reshape(exp_total, capacity)
    back_rows, back_weight = (
        lax.all_to_all(
            rows_stack.astype(jnp.bfloat16), "seq", split_axis=0, concat_axis=0, tiled=True
        ).astype(rows_stack.dtype),
        lax.all_to_all(
            weight_stack.astype(jnp.bfloat16), "seq", split_axis=0, concat_axis=0, tiled=True
        ).astype(weight_stack.dtype),
    )
    combined = lax.dot_general(
        mover.astype(jnp.float32),
        back_rows.reshape(slot_total, back_rows.shape[2]),
        (((0,), (0,)), ((), ())),
        precision=lax.Precision.HIGHEST,
        preferred_element_type=jnp.float32,
    )
    pairing_weight = lax.dot_general(
        placing.astype(jnp.float32),
        back_weight.reshape(slot_total),
        (((0,), (0,)), ((), ())),
        precision=lax.Precision.HIGHEST,
        preferred_element_type=jnp.float32,
    )
    normed_gradient_piece = lax.psum_scatter(
        combined.astype(jnp.bfloat16), "dp", scatter_dimension=1, tiled=True
    ).astype(jnp.float32)
    standardized_piece = token_piece * reciprocal_root_mean[:, None]
    correction_term = normed_gradient_piece * gain_part[None, :]
    stat_sum, grad_weights = lax.psum(
        (
            jnp.sum(correction_term * standardized_piece, axis=1),
            pairing_weight.reshape(token_row_list, picked_count),
        ),
        "dp",
    )
    reduced_statistic = stat_sum / width
    token_gradient = (
        upstream.astype(jnp.float32)
        + reciprocal_root_mean[:, None]
        * (correction_term - standardized_piece * reduced_statistic[:, None])
    ).astype(jnp.bfloat16)
    gain_gradient = lax.psum(jnp.sum(normed_gradient_piece * standardized_piece, axis=0), "seq")
    grad_gate_up = jnp.stack(grads_gu, axis=0)
    grad_down = jnp.stack(grads_dn, axis=0)
    return (token_gradient, gain_gradient, grad_weights, grad_gate_up, grad_down)


def solution(mesh):
    in_specs = (
        P("seq", "dp"),
        P("seq", "dp"),
        P(),
        P("seq", None),
        P("seq", None),
        P("seq", None, None, "dp"),
        P("seq", "dp", None),
    )
    out_specs = (
        P("seq", "dp"),
        P("dp"),
        P("seq", None),
        P("seq", None, None, "dp"),
        P("seq", "dp", None),
    )
    return jax.shard_map(body, mesh=mesh, in_specs=in_specs, out_specs=out_specs, check_vma=False)
```

profile of v0, /device:TPU:0, one launch (start us, length us, event | category | flops | bytes accessed | tf_op | source)
XLA Modules:
  0.0 320.5 jit_solution(3997811425725666372)
XLA Ops:
  11.7 5.2 %all-to-all-start = ((bf16[8,2,48]{2,1,0:T(2,128)(2,1)}), bf16[8,2,48]{2,1,0:T(2,128)(2,1)S(1)}, u32[]{:S(2)}, u32[]{:S(2)}) async-start(bf16[8,2,48]{2,1,0:T(2,128)(2,1)} %all_to_all.19), calls=%async_computation | async-start | bytes 8192 | tf_op jit(solution)/shard_map/all_to_all | solution.py:97
  18.6 19.5 %all_gather.6 = bf16[128,2880]{0,1:T(8,128)(2,1)S(1)} all-gather(bf16[128,720]{0,1:T(8,128)(2,1)} %param.7), channel_id=1, replica_groups=mesh['dp'=4,'seq'=8] {'dp'}, dimensions={1}, use_global_device_ids=true | all-gather | bytes 921600 | tf_op jit(solution)/shard_map/all_gather | solution.py:69
  38.5 3.4 %convolution_convert_fusion = bf16[768,2880]{0,1:T(8,128)(2,1)} fusion(bf16[768,128]{1,0:T(8,128)(2,1)S(1)} %fusion.21, bf16[128,2880]{0,1:T(8,128)(2,1)S(1)} %all_gather.6, f32[2880]{0:T(1024)S(1)} %convert_element_type.124, f32[128]{0:T(128)S(1)} %add_rsqrt_fusion), kind=kOutput, calls=%fused_computation.1 | convolution fusion | flops 569917440 | bytes 5369600 | tf_op jit(solution)/shard_map/dot_general | solution.py:77
  41.9 6.5 %copy.111 = bf16[768,2880]{1,0:T(8,128)(2,1)} copy(bf16[768,2880]{0,1:T(8,128)(2,1)} %convolution_convert_fusion) | data formatting | bytes 8847360 | tf_op jit(solution)/shard_map/convert_element_type | solution.py:77
  48.4 4.7 %all-to-all-start.2 = ((bf16[16,48,2880]{2,1,0:T(8,128)(2,1)}), bf16[16,48,2880]{2,1,0:T(8,128)(2,1)}, u32[]{:S(2)}, u32[]{:S(2)}) async-start(bf16[16,48,2880]{2,1,0:T(8,128)(2,1)} %bitcast.106), calls=%async_computation.2 | async-start | bytes 9043968 | tf_op jit(solution)/shard_map/all_to_all | solution.py:83
  53.1 17.6 %all_gather.7 = bf16[128,2880]{0,1:T(8,128)(2,1)S(1)} all-gather(bf16[128,720]{0,1:T(8,128)(2,1)S(1)} %copy-done.9), channel_id=1, replica_groups=mesh['dp'=4,'seq'=8] {'dp'}, dimensions={1}, use_global_device_ids=true | all-gather | bytes 921600 | tf_op jit(solution)/shard_map/all_gather | solution.py:70
  70.7 3.5 %convolution_convert_fusion.1 = bf16[768,2880]{0,1:T(8,128)(2,1)} fusion(bf16[768,128]{1,0:T(8,128)(2,1)S(1)} %fusion.21, bf16[128,2880]{0,1:T(8,128)(2,1)S(1)} %all_gather.7), kind=kOutput, calls=%fused_computation.2 | convolution fusion | flops 568442880 | bytes 5357568 | tf_op jit(solution)/shard_map/dot_general | solution.py:80
  74.2 6.6 %copy.109 = bf16[768,2880]{1,0:T(8,128)(2,1)} copy(bf16[768,2880]{0,1:T(8,128)(2,1)} %convolution_convert_fusion.1) | data formatting | bytes 8847360 | tf_op jit(solution)/shard_map/convert_element_type | solution.py:80
  80.8 25.0 %all-to-all-done.2 = bf16[16,48,2880]{2,1,0:T(8,128)(2,1)} async-done(((bf16[16,48,2880]{2,1,0:T(8,128)(2,1)}), bf16[16,48,2880]{2,1,0:T(8,128)(2,1)}, u32[]{:S(2)}, u32[]{:S(2)}) %all-to-all-start.2) | async-done | bytes 4423712 | tf_op jit(solution)/shard_map/all_to_all | solution.py:83
  105.8 4.8 %all-to-all-start.1 = ((bf16[16,48,2880]{2,1,0:T(8,128)(2,1)}), bf16[16,48,2880]{2,1,0:T(8,128)(2,1)}, u32[]{:S(2)}, u32[]{:S(2)}) async-start(bf16[16,48,2880]{2,1,0:T(8,128)(2,1)} %bitcast.105), calls=%async_computation.1 | async-start | bytes 9043968 | tf_op jit(solution)/shard_map/all_to_all | solution.py:90
  110.6 5.9 %fusion.55 = (bf16[1,2880,2,360]{1,3,2,0:T(8,128)(2,1)}, bf16[1,2880,2,360]{1,3,2,0:T(8,128)(2,1)}) fusion(bf16[2,2880,2,360]{1,3,2,0:T(8,128)(2,1)} %param.12), kind=kLoop, calls=%fused_computation.103 | loop fusion | bytes 16588800 | tf_op jit(solution)/shard_map/slice | solution.py:116
  116.7 4.7 %fusion.56 = (bf16[8,1,48,2880]{3,2,1,0:T(8,128)(2,1)}, bf16[8,1,48,2880]{3,2,1,0:T(8,128)(2,1)}) fusion(bf16[8,2,48,2880]{3,2,1,0:T(8,128)(2,1)} %bitcast.6), kind=kLoop, calls=%fused_computation.104 | loop fusion | bytes 8847360 | tf_op jit(solution)/shard_map/slice | solution.py:113
  121.4 41.7 %all-to-all-done.1 = bf16[16,48,2880]{2,1,0:T(8,128)(2,1)} async-done(((bf16[16,48,2880]{2,1,0:T(8,128)(2,1)}), bf16[16,48,2880]{2,1,0:T(8,128)(2,1)}, u32[]{:S(2)}, u32[]{:S(2)}) %all-to-all-start.1) | async-done | bytes 4423712 | tf_op jit(solution)/shard_map/all_to_all | solution.py:90
  163.0 2.8 fusion.57
  168.5 2.5 fusion.59
  175.1 5.3 %fusion.58 = f32[384,720]{0,1:T(8,128)S(1)} fusion(bf16[384,2880]{1,0:T(8,128)(2,1)} %bitcast.115, bf16[2880,720]{0,1:T(8,128)(2,1)} %bitcast.107), kind=kOutput, calls=%fused_computation.106 | convolution fusion | flops 1592524800 | bytes 7464960 | tf_op jit(solution)/shard_map/dot_general | solution.py:11
  180.4 4.0 %fusion.33 = (bf16[384]{0:T(512)(128)(2,1)S(1)}, bf16[384,360]{0,1:T(8,128)(2,1)}, bf16[384,360]{0,1:T(8,128)(2,1)S(1)}, bf16[384,360]{0,1:T(8,128)(2,1)}) fusion(f32[384,720]{0,1:T(8,128)S(1)} %fusion.58, f32[384]{0:T(512)S(1)} %reshape.176, bf16[384,2880]{1,0:T(8,128)(2,1)S(1)} %bitcast.111, bf16[2,360,2880]{2,1,0:T(8,128)(2,1)} %param.13), kind=kOutput, calls=%fused_computation.52 | convolution fusion | flops 799165056 | bytes 6269184 | tf_op jit(solution)/shard_map/dot_general | solution.py:17
  185.8 4.4 %fusion.3 = bf16[8,1,48,2880]{3,2,0,1:T(8,128)(2,1)S(1)} fusion(bf16[2880,720,1]{0,1,2:T(8,128)(2,1)} %bitcast.109, bf16[8,48,360]{2,1,0:T(8,128)(2,1)} %bitcast.121, bf16[8,48,360]{2,1,0:T(8,128)(2,1)} %bitcast.122), kind=kOutput, calls=%fused_computation.14 | convolution fusion | flops 1594736640 | bytes 6912000 | tf_op jit(solution)/shard_map/dot_general | solution.py:33
  190.2 4.2 %fusion.2 = bf16[8,1,48,2880]{3,2,0,1:T(8,128)(2,1)S(1)} fusion(bf16[2880,720,1]{0,1,2:T(8,128)(2,1)} %bitcast.108, bf16[8,48,360]{2,1,0:T(8,128)(2,1)S(1)} %bitcast.123, bf16[8,48,360]{2,1,0:T(8,128)(2,1)S(1)} %bitcast.124), kind=kOutput, calls=%fused_computation.13 | convolution fusion | flops 1594736640 | bytes 6912000 | tf_op jit(solution)/shard_map/dot_general | solution.py:33
  197.4 4.9 %all-to-all-start.3 = ((bf16[16,48,2880]{2,1,0:T(8,128)(2,1)}), bf16[16,48,2880]{2,1,0:T(8,128)(2,1)}, u32[]{:S(2)}, u32[]{:S(2)}) async-start(bf16[16,48,2880]{2,1,0:T(8,128)(2,1)} %bitcast.104), calls=%async_computation.3 | async-start | bytes 9043968 | tf_op jit(solution)/shard_map/all_to_all | solution.py:124
  204.3 3.8 %fusion.5 = bf16[1,360,2880]{2,1,0:T(8,128)(2,1)} fusion(bf16[384,2880]{1,0:T(8,128)(2,1)S(1)} %bitcast.118, bf16[384,360]{0,1:T(8,128)(2,1)} %get-tuple-element.14, f32[384]{0:T(512)S(1)} %reshape.177), kind=kOutput, calls=%fused_computation.16 | convolution fusion | flops 797713920 | bytes 4563456 | tf_op jit(solution)/shard_map/dot_general | solution.py:27
  208.1 4.4 %fusion = bf16[1,2880,2,360]{1,3,2,0:T(8,128)(2,1)} fusion(bf16[384,2880,1]{1,0,2:T(8,128)(2,1)S(1)} %bitcast.116, bf16[2,360,384]{2,1,0:T(8,128)(2,1)S(1)} %bitcast.120), kind=kOutput, calls=%fused_computation.6 | convolution fusion | flops 1594598400 | bytes 6912000 | tf_op jit(solution)/shard_map/dot_general | solution.py:30
  212.5 4.4 %fusion.1 = bf16[1,2880,2,360]{1,3,2,0:T(8,128)(2,1)} fusion(bf16[384,2880,1]{1,0,2:T(8,128)(2,1)S(1)} %bitcast.114, bf16[2,360,384]{2,1,0:T(8,128)(2,1)S(1)} %bitcast.119), kind=kOutput, calls=%fused_computation.7 | convolution fusion | flops 1594598400 | bytes 6912000 | tf_op jit(solution)/shard_map/dot_general | solution.py:30
  217.0 37.7 %all-to-all-done.3 = bf16[16,48,2880]{2,1,0:T(8,128)(2,1)} async-done(((bf16[16,48,2880]{2,1,0:T(8,128)(2,1)}), bf16[16,48,2880]{2,1,0:T(8,128)(2,1)}, u32[]{:S(2)}, u32[]{:S(2)}) %all-to-all-start.3) | async-done | bytes 4423712 | tf_op jit(solution)/shard_map/all_to_all | solution.py:124
  254.7 3.3 %all-to-all-start.4 = ((bf16[8,2,48]{2,1,0:T(2,128)(2,1)}), bf16[8,2,48]{2,1,0:T(2,128)(2,1)S(1)}, u32[]{:S(2)}, u32[]{:S(2)}) async-start(bf16[8,2,48]{2,1,0:T(2,128)(2,1)} %copy.120), calls=%async_computation.5 | async-start | bytes 8192 | tf_op jit(solution)/shard_map/all_to_all | solution.py:127
  258.1 5.1 %convolution_convert_fusion.8 = bf16[128,2880]{0,1:T(8,128)(2,1)} fusion(bf16[768,128]{1,0:T(8,128)(2,1)S(1)} %fusion.21, bf16[768,2880]{1,0:T(8,128)(2,1)} %bitcast.22), kind=kOutput, calls=%fused_computation.17 | convolution fusion | flops 566599680 | bytes 5357568 | tf_op jit(solution)/shard_map/dot_general | solution.py:131
  263.2 4.5 %fusion.4 = bf16[1,360,2880]{2,1,0:T(8,128)(2,1)} fusion(bf16[384,2880]{1,0:T(8,128)(2,1)} %bitcast.112, bf16[384,360]{0,1:T(8,128)(2,1)S(1)} %copy-done.11, f32[384]{0:T(512)S(1)} %reshape.176), kind=kOutput, calls=%fused_computation.15 | convolution fusion | flops 797713920 | bytes 4563456 | tf_op jit(solution)/shard_map/dot_general | solution.py:27
  267.7 6.6 %pad_maximum_fusion = bf16[2,2880,2,360]{1,3,2,0:T(8,128)(2,1)} fusion(bf16[1,2880,2,360]{1,3,2,0:T(8,128)(2,1)} %fusion.1, bf16[1,2880,2,360]{1,3,2,0:T(8,128)(2,1)S(1)} %copy-done.1), kind=kLoop, calls=%fused_computation | loop fusion | flops 4147200 | bytes 16588800 | tf_op jit(solution)/shard_map/stack | solution.py:164
  274.3 4.8 %pad_maximum_fusion.2 = bf16[2,360,2880]{2,1,0:T(8,128)(2,1)} fusion(bf16[1,360,2880]{2,1,0:T(8,128)(2,1)} %fusion.5, bf16[1,360,2880]{2,1,0:T(8,128)(2,1)} %fusion.4), kind=kLoop, calls=%fused_computation.8 | loop fusion | flops 2073600 | bytes 8294400 | tf_op jit(solution)/shard_map/stack | solution.py:165
  279.6 6.5 %reduce-scatter.2.cloned.1.call-done = bf16[128,720]{0,1:T(8,128)(2,1)} async-done(((bf16[128,2880]{0,1:T(8,128)(2,1)}), bf16[128,720]{0,1:T(8,128)(2,1)}) %reduce-scatter.2.cloned.1.call-update) | async-done | bytes 184336 | tf_op jit(solution)/shard_map/reduce_scatter | solution.py:145
  287.4 12.8 %psum.22 = f32[720]{0:T(1024)} all-reduce(f32[720]{0:T(1024)S(1)} %get-tuple-element.5), channel_id=1, replica_groups=mesh['dp'=4,'seq'=8] {'seq'}, use_global_device_ids=true, to_apply=%region_9.10 | all-reduce | flops 720 | bytes 5760 | tf_op jit(solution)/shard_map/psum | solution.py:163
  300.2 11.7 %all-reduce = (f32[128]{0:T(128)S(1)}, f32[128,4]{0,1:T(4,128)}) all-reduce(f32[128]{0:T(128)S(1)} %get-tuple-element.6, f32[128,4]{0,1:T(4,128)S(1)} %bitcast.125), channel_id=1, replica_groups=mesh['dp'=4,'seq'=8] {'dp'}, use_global_device_ids=true, to_apply=%region_7.8 | all-reduce | flops 640 | bytes 5120 | tf_op jit(solution)/shard_map/psum | solution.py:150
  (76 shorter events, 23.4 us)
Async XLA Ops:
  11.7 36.7 %all-to-all-start = ((bf16[8,2,48]{2,1,0:T(2,128)(2,1)}), bf16[8,2,48]{2,1,0:T(2,128)(2,1)S(1)}, u32[]{:S(2)}, u32[]{:S(2)}) async-start(bf16[8,2,48]{2,1,0:T(2,128)(2,1)} %all_to_all.19), calls=%async_computation | async-start | bytes 8192 | tf_op jit(solution)/shard_map/all_to_all | solution.py:97
  48.4 4.7 %copy-start.9 = (bf16[128,720]{0,1:T(8,128)(2,1)S(1)}, bf16[128,720]{0,1:T(8,128)(2,1)}, u32[]{:S(2)}) copy-start(bf16[128,720]{0,1:T(8,128)(2,1)} %param.8) | copy-start | bytes 552964
  48.4 57.3 %all-to-all-start.2 = ((bf16[16,48,2880]{2,1,0:T(8,128)(2,1)}), bf16[16,48,2880]{2,1,0:T(8,128)(2,1)}, u32[]{:S(2)}, u32[]{:S(2)}) async-start(bf16[16,48,2880]{2,1,0:T(8,128)(2,1)} %bitcast.106), calls=%async_computation.2 | async-start | bytes 9043968 | tf_op jit(solution)/shard_map/all_to_all | solution.py:83
  105.8 57.3 %all-to-all-start.1 = ((bf16[16,48,2880]{2,1,0:T(8,128)(2,1)}), bf16[16,48,2880]{2,1,0:T(8,128)(2,1)}, u32[]{:S(2)}, u32[]{:S(2)}) async-start(bf16[16,48,2880]{2,1,0:T(8,128)(2,1)} %bitcast.105), calls=%async_computation.1 | async-start | bytes 9043968 | tf_op jit(solution)/shard_map/all_to_all | solution.py:90
  163.0 3.6 %copy-start = (bf16[1,2880,2,360]{1,3,2,0:T(8,128)(2,1)S(1)}, bf16[1,2880,2,360]{1,3,2,0:T(8,128)(2,1)}, u32[]{:S(2)}) copy-start(bf16[1,2880,2,360]{1,3,2,0:T(8,128)(2,1)} %get-tuple-element.16) | copy-start | bytes 12441604
  163.0 5.5 %copy-start.3 = (bf16[8,1,48,2880]{3,2,1,0:T(8,128)(2,1)S(1)}, bf16[8,1,48,2880]{3,2,1,0:T(8,128)(2,1)}, u32[]{:S(2)}) copy-start(bf16[8,1,48,2880]{3,2,1,0:T(8,128)(2,1)} %get-tuple-element.18) | copy-start | bytes 6635524
  163.0 8.0 %slice-start = ((s8[4239360]{0:T(1024)(128)(4,1)}), s8[4194304]{0:T(1024)(128)(4,1)S(1)}, s32[]{:S(2)}) async-start(s8[4239360]{0:T(1024)(128)(4,1)} %bitcast.126), calls=%async_computation.7 | async-start | bytes 8388608
  165.8 5.2 %copy-start.6 = (bf16[8,1,48,2880]{3,2,1,0:T(8,128)(2,1)}, bf16[8,1,48,2880]{3,2,1,0:T(8,128)(2,1)S(1)}, u32[]{:S(2)}) copy-start(bf16[8,1,48,2880]{3,2,1,0:T(8,128)(2,1)S(1)} %get-tuple-element.20) | copy-start | bytes 6635524
  165.8 14.6 %copy-start.2 = (bf16[8,1,48,2880]{3,2,1,0:T(8,128)(2,1)}, bf16[8,1,48,2880]{3,2,1,0:T(8,128)(2,1)S(1)}, u32[]{:S(2)}) copy-start(bf16[8,1,48,2880]{3,2,1,0:T(8,128)(2,1)S(1)} %get-tuple-element.19) | copy-start | bytes 6635524
  168.5 2.5 slice-start.1
  197.4 4.9 %copy-start.10 = (bf16[2880]{0:T(1024)(128)(2,1)S(1)}, bf16[2880]{0:T(1024)(128)(2,1)}, u32[]{:S(2)}) copy-start(bf16[2880]{0:T(1024)(128)(2,1)} %param.9) | copy-start | bytes 17284
  197.4 57.3 %all-to-all-start.3 = ((bf16[16,48,2880]{2,1,0:T(8,128)(2,1)}), bf16[16,48,2880]{2,1,0:T(8,128)(2,1)}, u32[]{:S(2)}, u32[]{:S(2)}) async-start(bf16[16,48,2880]{2,1,0:T(8,128)(2,1)} %bitcast.104), calls=%async_computation.3 | async-start | bytes 9043968 | tf_op jit(solution)/shard_map/all_to_all | solution.py:124
  202.3 2.0 copy-start.7
  204.3 3.8 %copy-start.5 = (bf16[8,1,48,2880]{3,2,1,0:T(8,128)(2,1)S(1)}, bf16[8,1,48,2880]{3,2,1,0:T(8,128)(2,1)}, u32[]{:S(2)}) copy-start(bf16[8,1,48,2880]{3,2,1,0:T(8,128)(2,1)} %get-tuple-element.17) | copy-start | bytes 6635524
  208.1 4.4 %copy-start.4 = (bf16[8,1,48,2880]{3,2,1,0:T(8,128)(2,1)S(1)}, bf16[8,1,48,2880]{3,2,1,0:T(8,128)(2,1)}, u32[]{:S(2)}) copy-start(bf16[8,1,48,2880]{3,2,1,0:T(8,128)(2,1)} %get-tuple-element.18) | copy-start | bytes 6635524
  254.7 24.4 %all-to-all-start.4 = ((bf16[8,2,48]{2,1,0:T(2,128)(2,1)}), bf16[8,2,48]{2,1,0:T(2,128)(2,1)S(1)}, u32[]{:S(2)}, u32[]{:S(2)}) async-start(bf16[8,2,48]{2,1,0:T(2,128)(2,1)} %copy.120), calls=%async_computation.5 | async-start | bytes 8192 | tf_op jit(solution)/shard_map/all_to_all | solution.py:127
  258.0 28.1 %reduce-scatter.2.cloned.1.call-start = ((), (), s32[]{:S(2)}) async-start(), calls=%async_computation.6 | async-start | bytes 921600 | tf_op jit(solution)/shard_map/reduce_scatter | solution.py:145
  258.1 5.1 %copy-start.11 = (bf16[384,360]{0,1:T(8,128)(2,1)S(1)}, bf16[384,360]{0,1:T(8,128)(2,1)}, u32[]{:S(2)}) copy-start(bf16[384,360]{0,1:T(8,128)(2,1)} %get-tuple-element.12) | copy-start | bytes 829444
  263.2 4.5 %copy-start.1 = (bf16[1,2880,2,360]{1,3,2,0:T(8,128)(2,1)S(1)}, bf16[1,2880,2,360]{1,3,2,0:T(8,128)(2,1)}, u32[]{:S(2)}) copy-start(bf16[1,2880,2,360]{1,3,2,0:T(8,128)(2,1)} %fusion) | copy-start | bytes 12441604
  274.3 11.9 %copy-start.8 = (bf16[128,720]{0,1:T(8,128)(2,1)S(1)}, bf16[128,720]{0,1:T(8,128)(2,1)}, u32[]{:S(2)}) copy-start(bf16[128,720]{0,1:T(8,128)(2,1)} %param.7) | copy-start | bytes 552964
Sparse Core Ops, SparseCore 0:
  263.3 22.8 reduce-scatter.1
where the time goes:
time: 322 us; the launch traced here: 320 us
  waiting for transfers between devices  111 us (34%)
  blocking collectives  61.5 us (19%)
  matrix products  52.6 us (16%)
  local copies, waits for them, and re-layouts  38.9 us (12%)
  starting transfers between devices  23 us (7%)
  other arithmetic  19.3 us (6%)
  between operations  14.3 us (4%)
    all_to_all x1, waiting for transfers between devices, body(): lax.all_to_all(send_dy.reshape(exp_total, capacity, feat_width), 'seq', s...  41.7 us
    all_to_all x1, waiting for transfers between devices, body(): lax.all_to_all(rows_stack.astype(jnp.bfloat16), 'seq', split_axis=0, conc...  37.7 us
    all_to_all x1, waiting for transfers between devices, body(): lax.all_to_all(send_tok.reshape(exp_total, capacity, feat_width), 'seq',...  25 us
    all_gather x1, blocking collectives, body(): lax.all_gather(tokens, 'dp', axis=1, tiled=True)  19.5 us
    all_gather x1, blocking collectives, body(): lax.all_gather(upstream, 'dp', axis=1, tiled=True)  17.6 us
    psum x1, blocking collectives, body(): lax.psum(jnp.sum(normed_gradient_piece * standardized_piece, axis=0), 'seq')  12.8 us
    psum x1, blocking collectives, body(): lax.psum((jnp.sum(correction_term * standardized_piece, axis=1), pairing_...  11.7 us
    dot_general x2, matrix products, expert_terms(): lax.dot_general(x_rows, dproj, (((0,), (0,)), ((), ())), preferred_elemen...  8.88 us
  transfers between devices with their start and end apart: 6, of which 4 were waited for; matrix products, arithmetic and copies ran while one was open for 22% of the time, Pallas kernels for 0%

commit v1 on v0

--- a/solution.py
+++ b/solution.py
@@ -1,6 +1,8 @@
 import jax
 import jax.numpy as jnp
 from jax import lax
+from jax.experimental import pallas as pl
+from jax.experimental.pallas import tpu as pltpu
 from jax.sharding import PartitionSpec as P
 
 
@@ -35,6 +37,332 @@
     )
     return (grad_gu, grad_dn, grad_rows, weight_grad)
 
+
+def earlier_same(pairs):
+    count = pairs.shape[-1]
+    same = pairs[..., :, None] == pairs[..., None, :]
+    order = jnp.arange(count, dtype=jnp.int32)
+    before = order[None, :] < order[:, None]
+    return jnp.sum((same & before).astype(jnp.int32), axis=-1)
+
+
+def plane_neighbours(me):
+    core = me + 1 - 2 * (me % 2)
+    across_x = me + 2 - 4 * ((me // 2) % 2)
+    across_y = me + 4 - 8 * (me // 4)
+    return core, across_x, across_y
+
+
+def spread_kernel(depth, own_ref, out_ref, send_sem, recv_sem, copy_sem):
+    z = lax.axis_index("dp")
+    me = lax.axis_index("seq")
+    core, ax, ay = plane_neighbours(me)
+    diag = me + (ax - me) + (ay - me)
+
+    barrier = pltpu.get_barrier_semaphore()
+    for near in (core, ax, ay):
+        pl.semaphore_signal(barrier, inc=1, device_id={"seq": near})
+    for k in range(1, depth):
+        pl.semaphore_signal(barrier, inc=1, device_id={"dp": (z + k) % depth})
+    pl.semaphore_wait(barrier, 3 + depth - 1)
+
+    kinds = 9
+    started = {}
+
+    def send(index, source, target, where):
+        copy = pltpu.make_async_remote_copy(
+            src_ref=source,
+            dst_ref=target,
+            send_sem=send_sem.at[index],
+            recv_sem=recv_sem.at[index],
+            device_id=where,
+        )
+        copy.start()
+        started[index] = copy
+
+    def origin(k):
+        return (z + depth - k) % depth
+
+    def arrived(k, kind):
+        started[k * kinds + kind].wait_recv()
+
+    def own(k):
+        block = own_ref if k == 0 else out_ref.at[me, origin(k)]
+        if k > 0:
+            started[kinds * depth + k].wait_recv()
+        target = out_ref.at[me, origin(k)]
+        send(k * kinds + 0, block, target, {"seq": ax})
+        send(k * kinds + 1, block, target, {"seq": ay})
+        send(k * kinds + 2, block, target, {"seq": core})
+
+    def relay(k):
+        zs = origin(k)
+        arrived(k, 0)
+        from_x = out_ref.at[ax, zs]
+        send(k * kinds + 3, from_x.at[0], from_x.at[0], {"seq": ay})
+        arrived(k, 1)
+        from_y = out_ref.at[ay, zs]
+        send(k * kinds + 4, from_y.at[1], from_y.at[1], {"seq": ax})
+        send(k * kinds + 5, from_x, from_x, {"seq": core})
+        send(k * kinds + 6, from_y, from_y, {"seq": core})
+
+    def corner(k):
+        zs = origin(k)
+        far = out_ref.at[diag, zs]
+        arrived(k, 3)
+        send(k * kinds + 7, far.at[0], far.at[0], {"seq": core})
+        arrived(k, 4)
+        send(k * kinds + 8, far.at[1], far.at[1], {"seq": core})
+
+    for k in range(1, depth):
+        send(kinds * depth + k, own_ref, out_ref.at[me, z], {"dp": (z + k) % depth})
+    keep = pltpu.make_async_copy(own_ref, out_ref.at[me, z], copy_sem)
+    keep.start()
+    for step in range(depth + 2):
+        if step < depth:
+            own(step)
+        if 1 <= step <= depth:
+            relay(step - 1)
+        if 2 <= step:
+            corner(step - 2)
+    for k in range(depth):
+        for kind in (2, 5, 6, 7, 8):
+            arrived(k, kind)
+    for copy in started.values():
+        copy.wait_send()
+    keep.wait()
+
+
+def spread(block, depth, peers):
+    count = 9 * depth + depth
+    return pl.pallas_call(
+        lambda *refs: spread_kernel(depth, *refs),
+        out_shape=jax.ShapeDtypeStruct((peers, depth) + block.shape, block.dtype),
+        in_specs=[pl.BlockSpec(memory_space=pl.ANY)],
+        out_specs=pl.BlockSpec(memory_space=pl.ANY),
+        scratch_shapes=[
+            pltpu.SemaphoreType.DMA((count,)),
+            pltpu.SemaphoreType.DMA((count,)),
+            pltpu.SemaphoreType.DMA,
+        ],
+        compiler_params=pltpu.CompilerParams(collective_id=0, has_side_effects=True),
+        name="spread",
+    )(block)
+
+
+def fill_kernel(depth, part, got_ref, select_ref, gain_ref, x_ref, dy_ref):
+    members, _, capacity, _ = x_ref.shape
+    select = select_ref[0]
+    total = None
+    for z in range(depth):
+        piece = got_ref[0, z, 0, :, :part].astype(jnp.float32)
+        square = jnp.sum(piece * piece, axis=1, keepdims=True)
+        total = square if total is None else total + square
+    inv = lax.rsqrt(total / (part * depth) + 1e-05)
+    for z in range(depth):
+        at = slice(z * part, (z + 1) * part)
+        piece = got_ref[0, z, 0, :, :part].astype(jnp.float32)
+        normed = (piece * inv * gain_ref[:, at]).astype(jnp.bfloat16)
+        for source, target in ((normed, x_ref), (got_ref[0, z, 1, :, :part], dy_ref)):
+            chosen = jnp.dot(select, source, preferred_element_type=jnp.float32).astype(
+                jnp.bfloat16
+            )
+            for m in range(members):
+                target[m, 0, :, at] = chosen[m * capacity : (m + 1) * capacity]
+
+
+def fill_slots(got, select, gain, part, members, capacity):
+    peers, depth, _, rows, lanes = got.shape
+    width = part * depth
+    made = jax.ShapeDtypeStruct((members, peers, capacity, width), jnp.bfloat16)
+    out = pl.BlockSpec((members, 1, capacity, width), lambda b: (0, b, 0, 0))
+    return pl.pallas_call(
+        lambda *refs: fill_kernel(depth, part, *refs),
+        grid=(peers,),
+        out_shape=(made, made),
+        in_specs=[
+            pl.BlockSpec((1, depth, 2, rows, lanes), lambda b: (b, 0, 0, 0, 0)),
+            pl.BlockSpec((1,) + select.shape[1:], lambda b: (b, 0, 0)),
+            pl.BlockSpec((1, width), lambda b: (0, 0)),
+        ],
+        out_specs=(out, out),
+        compiler_params=pltpu.CompilerParams(vmem_limit_bytes=32 * 2**20),
+        name="fill_slots",
+    )(got, select, gain[None, :])
+
+
+def exchange_kernel(depth, peers, stat_ref, gain_ref, stats_ref, gains_ref, sends, lands, keeps):
+    z = lax.axis_index("dp")
+    me = lax.axis_index("seq")
+    barrier = pltpu.get_barrier_semaphore()
+    for k in range(1, depth):
+        pl.semaphore_signal(barrier, inc=1, device_id={"dp": (z + k) % depth})
+    for k in range(1, peers):
+        pl.semaphore_signal(barrier, inc=1, device_id={"seq": (me + k) % peers})
+    pl.semaphore_wait(barrier, depth + peers - 2)
+    copies = []
+    for k in range(1, depth):
+        where = {"dp": (z + k) % depth}
+        copies.append((stat_ref, stats_ref.at[k], where))
+    for k in range(1, peers):
+        where = {"seq": (me + k) % peers}
+        copies.append((gain_ref, gains_ref.at[k], where))
+    running = []
+    for n, (source, target, where) in enumerate(copies):
+        copy = pltpu.make_async_remote_copy(
+            src_ref=source,
+            dst_ref=target,
+            send_sem=sends.at[n],
+            recv_sem=lands.at[n],
+            device_id=where,
+        )
+        copy.start()
+        running.append(copy)
+    for n, (source, target) in enumerate(((stat_ref, stats_ref), (gain_ref, gains_ref))):
+        copy = pltpu.make_async_copy(source, target.at[0], keeps.at[n])
+        copy.start()
+        running.append(copy)
+    for copy in running:
+        copy.wait()
+
+
+def exchange(stat, gain, depth, peers):
+    count = depth + peers - 2
+    return pl.pallas_call(
+        lambda *refs: exchange_kernel(depth, peers, *refs),
+        out_shape=(
+            jax.ShapeDtypeStruct((depth,) + stat.shape, stat.dtype),
+            jax.ShapeDtypeStruct((peers,) + gain.shape, gain.dtype),
+        ),
+        in_specs=[pl.BlockSpec(memory_space=pltpu.VMEM)] * 2,
+        out_specs=(pl.BlockSpec(memory_space=pltpu.VMEM),) * 2,
+        scratch_shapes=[
+            pltpu.SemaphoreType.DMA((count,)),
+            pltpu.SemaphoreType.DMA((count,)),
+            pltpu.SemaphoreType.DMA((2,)),
+        ],
+        compiler_params=pltpu.CompilerParams(collective_id=1, has_side_effects=True),
+        name="exchange",
+    )(stat, gain)
+
+
+def plane_body(tokens, upstream, norm_gain, experts, route_weights, w_gate_up, w_down):
+    dp_count = lax.axis_size("dp")
+    seq_count = lax.axis_size("seq")
+    rows, part = tokens.shape
+    width = part * dp_count
+    top = experts.shape[1]
+    exp_local = w_gate_up.shape[0]
+    hidden = w_down.shape[1]
+    exp_total = exp_local * seq_count
+    capacity = rows * top * 3 // (2 * exp_total)
+    slots = exp_local * capacity
+    everyone = seq_count * rows
+    me = lax.axis_index("seq")
+    lanes = -(-(part + 2 * top) // 128) * 128
+    room = lanes - part - 2 * top
+    fill = jnp.zeros((rows, room), jnp.bfloat16)
+    mine = jnp.stack(
+        [
+            jnp.concatenate([tokens, experts.astype(jnp.bfloat16), route_weights, fill], axis=1),
+            jnp.concatenate(
+                [upstream, jnp.zeros((rows, 2 * top), jnp.bfloat16), fill], axis=1
+            ),
+        ]
+    )
+    got = spread(mine, dp_count, seq_count)
+    all_experts = got[:, 0, 0, :, part : part + top].astype(jnp.int32).reshape(seq_count, -1)
+    all_weights = got[:, 0, 0, :, part + top : part + 2 * top].reshape(seq_count, -1)
+    rank = earlier_same(all_experts)
+
+    gain = norm_gain.astype(jnp.float32)
+    own_tok = lax.dynamic_index_in_dim(got, me, 0, keepdims=False)[:, 0, :, :part].astype(
+        jnp.float32
+    )
+    my_inv = lax.rsqrt(jnp.sum(own_tok * own_tok, axis=(0, 2)) / width + 1e-05)[:, None]
+
+    local = all_experts - me * exp_local
+    place = jnp.where((local >= 0) & (local < exp_local), local * capacity + rank, -1)
+    place = place.reshape(seq_count, rows, top)
+    numbers = jnp.arange(slots, dtype=jnp.int32)
+    hits = jnp.swapaxes(place, 1, 2)[:, :, None, :] == numbers[None, None, :, None]
+    select = jnp.sum(hits.astype(jnp.float32), axis=1).astype(jnp.bfloat16)
+    weights = jnp.swapaxes(
+        all_weights.reshape(seq_count, rows, top).astype(jnp.float32), 1, 2
+    )
+    slot_weight = jnp.sum(jnp.where(hits, weights[:, :, None, :], 0.0), axis=(1, 3))
+    slot_weight = jnp.swapaxes(
+        slot_weight.astype(jnp.bfloat16).reshape(seq_count, exp_local, capacity), 0, 1
+    ).reshape(-1)
+    x_all, dy_all = fill_slots(got, select, gain, part, exp_local, capacity)
+    x_all = x_all.reshape(-1, width)
+    dy_all = dy_all.reshape(-1, width)
+    member_rows = seq_count * capacity
+    grads_gu, grads_dn, back_rows, back_weights = [], [], [], []
+    for member in range(exp_local):
+        at = slice(member * member_rows, (member + 1) * member_rows)
+        g_gu, g_dn, g_rows, g_weight = expert_terms(
+            x_all[at], dy_all[at], slot_weight[at], w_gate_up[member], w_down[member]
+        )
+        grads_gu.append(g_gu.reshape(width, 2, hidden).astype(jnp.bfloat16))
+        grads_dn.append(g_dn.astype(jnp.bfloat16))
+        back_rows.append(g_rows.astype(jnp.bfloat16).reshape(seq_count, capacity, width))
+        back_weights.append(g_weight.reshape(seq_count, capacity, 1))
+    high = [w.astype(jnp.bfloat16) for w in back_weights]
+    low = [(w - h.astype(jnp.float32)).astype(jnp.bfloat16) for w, h in zip(back_weights, high)]
+    leaving = jnp.concatenate(
+        [jnp.concatenate(t, axis=2) for t in zip(back_rows, high, low)], axis=1
+    )
+    home = lax.all_to_all(leaving, "seq", split_axis=0, concat_axis=0, tiled=True)
+    home = home.reshape(seq_count * slots, width + 2)
+    my_experts = experts.reshape(-1)
+    spot = (my_experts * capacity + earlier_same(my_experts)).reshape(rows, top)
+    mover = jnp.sum(
+        (spot[:, :, None] == jnp.arange(seq_count * slots, dtype=jnp.int32)).astype(jnp.float32),
+        axis=1,
+    ).astype(jnp.bfloat16)
+    combined = jnp.dot(mover, home[:, :width], preferred_element_type=jnp.float32)
+    came = home[:, width].astype(jnp.float32) + home[:, width + 1].astype(jnp.float32)
+    pair_weight = jnp.sum(
+        jnp.where(
+            spot[:, :, None] == jnp.arange(seq_count * slots, dtype=jnp.int32),
+            came[None, None, :],
+            0.0,
+        ),
+        axis=2,
+    )
+    dnormed = lax.psum_scatter(
+        combined.astype(jnp.bfloat16), "dp", scatter_dimension=1, tiled=True
+    ).astype(jnp.float32)
+    my_gain = lax.dynamic_slice_in_dim(gain, lax.axis_index("dp") * part, part, 0)
+    xhat = tokens.astype(jnp.float32) * my_inv
+    u = dnormed * my_gain[None, :]
+    small = jnp.concatenate([jnp.sum(u * xhat, axis=1)[:, None], pair_weight], axis=1)
+    tile = 8 * 128
+    stat_tiles = -(-small.size // tile)
+    stat_block = jnp.pad(small.T.reshape(-1), (0, stat_tiles * tile - small.size))
+    gain_part = jnp.sum(dnormed * xhat, axis=0)
+    gain_tiles = -(-part // tile)
+    gain_block = jnp.pad(gain_part, (0, gain_tiles * tile - part))
+    stat_all, gain_all = exchange(
+        stat_block.reshape(stat_tiles * 8, 128),
+        gain_block.reshape(gain_tiles * 8, 128),
+        dp_count,
+        seq_count,
+    )
+    both = jnp.sum(stat_all, axis=0).reshape(-1)[: small.size].reshape(1 + top, rows).T
+    gain_gradient = jnp.sum(gain_all, axis=0).reshape(-1)[:part]
+    stat = both[:, :1] / width
+    token_gradient = (upstream.astype(jnp.float32) + my_inv * (u - xhat * stat)).astype(
+        jnp.bfloat16
+    )
+    return (
+        token_gradient,
+        gain_gradient,
+        both[:, 1:],
+        jnp.stack(grads_gu, axis=0),
+        jnp.stack(grads_dn, axis=0),
+    )
 
 def body(tokens, upstream, norm_gain, experts, route_weights, w_gate_up, w_down):
     dp_count = lax.axis_size("dp")
@@ -53,10 +381,7 @@
     )
     token_piece = tokens.astype(jnp.float32)
     pair_experts = experts.reshape(-1)
-    onehot = (pair_experts[:, None] == jnp.arange(exp_total, dtype=jnp.int32)[None, :]).astype(
-        jnp.int32
-    )
-    rank = jnp.sum((jnp.cumsum(onehot, axis=0) - 1) * onehot, axis=1)
+    rank = earlier_same(pair_experts)
     position = pair_experts * capacity + rank
     placing = (position[None, :] == jnp.arange(slot_total, dtype=jnp.int32)[:, None]).astype(
         jnp.bfloat16
@@ -183,4 +508,5 @@
         P("seq", None, None, "dp"),
         P("seq", "dp", None),
     )
-    return jax.shard_map(body, mesh=mesh, in_specs=in_specs, out_specs=out_specs, check_vma=False)
+    fast = mesh.shape["seq"] == 8 and mesh.shape["dp"] > 1
+    return jax.shard_map(plane_body if fast else body, mesh=mesh, in_specs=in_specs, out_specs=out_specs, check_vma=False)

time: 322 us -> 271 us (0.84)
  Pallas kernels: 0 us -> 79.2 us
  blocking collectives: 61.5 us -> 0 us
  waiting for transfers between devices: 111 us -> 54.7 us
  starting transfers between devices: 23 us -> 4.79 us
  other arithmetic: 19.3 us -> 27.7 us
  matrix products: 52.6 us -> 47.4 us
    pallas_call x0 -> x3, Pallas kernels: none -> 79.2 us  [the longest x1 65.4 us: spread(): pl.pallas_call(lambda *refs: spread_kernel(depth, *refs), out_shape=jax.S...]
    all_to_all x5 -> x1, waiting for transfers between devices: 104 us -> 40.6 us  [plane_body(): lax.all_to_all(leaving, 'seq', split_axis=0, concat_axis=0, tiled=True)]
    all_gather x2 -> x0, blocking collectives: 37.1 us -> none  [the longest x1 19.5 us: body(): lax.all_gather(tokens, 'dp', axis=1, tiled=True)]
    psum x2 -> x0, blocking collectives: 24.5 us -> none  [the longest x1 12.8 us: body(): lax.psum(jnp.sum(normed_gradient_piece * standardized_piece, axis=0), 'seq')]
    all_to_all x5 -> x1, starting transfers between devices: 22.9 us -> 4.74 us  [plane_body(): lax.all_to_all(leaving, 'seq', split_axis=0, concat_axis=0, tiled=True)]
    concatenate x0 -> x4, local copies, waits for them, and re-layouts: none -> 7.84 us  [the longest x2 7.69 us: plane_body(): jnp.concatenate(t, axis=2)]
    dot_general x5 -> x1, matrix products: 12.8 us -> 4.99 us  [plane_body(): jnp.dot(mover, home[:, :width], preferred_element_type=jnp.float32)]
    reduce_scatter x1, waiting for transfers between devices: 6.54 us -> 14.1 us  [plane_body(): lax.psum_scatter(combined.astype(jnp.bfloat16), 'dp', scatter_dimension=1...]
  transfers between devices with their start and end apart: 6 -> 2, of which waited for: 4 -> 2; matrix products, arithmetic and copies ran while one was open for 22% -> 10% of each run, Pallas kernels for 0% -> 0%
where the time goes in v1:
time: 271 us; the launch traced here: 270 us
  Pallas kernels  79.2 us (29%)
  waiting for transfers between devices  54.7 us (20%)
  matrix products  47.4 us (17%)
  local copies, waits for them, and re-layouts  41.8 us (15%)
  other arithmetic  27.7 us (10%)
  between operations  14.4 us (5%)
  starting transfers between devices  4.79 us (2%)
    pallas_call x1, Pallas kernels, spread(): pl.pallas_call(lambda *refs: spread_kernel(depth, *refs), out_shape=jax.S...  65.4 us
    all_to_all x1, waiting for transfers between devices, plane_body(): lax.all_to_all(leaving, 'seq', split_axis=0, concat_axis=0, tiled=True)  40.6 us
    reduce_scatter x1, waiting for transfers between devices, plane_body(): lax.psum_scatter(combined.astype(jnp.bfloat16), 'dp', scatter_dimension=1...  14.1 us
    dot_general x2, matrix products, expert_terms(): lax.dot_general(dproj, flat_gu, (((1,), (1,)), ((), ())), preferred_eleme...  12.3 us
    dot_general x2, matrix products, expert_terms(): lax.dot_general(x_rows, dproj, (((0,), (0,)), ((), ())), preferred_elemen...  10.6 us
    unnamed x48, local copies, waits for them, and re-layouts  10.1 us
    dot_general x2, matrix products, expert_terms(): projected = jnp.dot(x_rows, flat_gu, preferred_element_type=jnp.float32)  7.95 us
    concatenate x2, local copies, waits for them, and re-layouts, plane_body(): jnp.concatenate(t, axis=2)  7.69 us
  transfers between devices with their start and end apart: 2, of which 2 were waited for; matrix products, arithmetic and copies ran while one was open for 10% of the time, Pallas kernels for 0%

profile of v1, /device:TPU:0, one launch (start us, length us, event | category | flops | bytes accessed | tf_op | source)
XLA Modules:
  0.0 270.0 jit_solution(14505053629875278716)
XLA Ops:
  13.3 5.9 %fusion.37 = (bf16[1,2880,2,360]{1,3,2,0:T(8,128)(2,1)}, bf16[1,2880,2,360]{1,3,2,0:T(8,128)(2,1)}) fusion(bf16[2,2880,2,360]{1,3,2,0:T(8,128)(2,1)} %param.12), kind=kLoop, calls=%fused_computation.96 | loop fusion | bytes 16588800 | tf_op jit(solution)/shard_map/slice | solution.py:305
  20.1 65.4 %spread.1.refs_0_ = bf16[8,4,2,128,768]{4,3,2,1,0:T(8,128)(2,1)} custom-call(bf16[2,128,768]{2,1,0:T(8,128)(2,1)} %pad_maximum_fusion.5.refs_0_), custom_call_target="tpu_custom_call" | custom-call | tf_op jit(solution)/shard_map/spread/pallas_call | solution.py:138
  85.6 1.4 slice_convert_fusion
  88.1 2.3 convert_reduce_fusion
  93.5 4.6 %copy-done = bf16[8,4,2,128,768]{4,3,2,1,0:T(8,128)(2,1)S(1)} copy-done((bf16[8,4,2,128,768]{4,3,2,1,0:T(8,128)(2,1)S(1)}, bf16[8,4,2,128,768]{4,3,2,1,0:T(8,128)(2,1)}, u32[]{:S(2)}) %copy-start) | copy-done | bytes 12582936
  98.0 6.8 %fill_slots.1 = (bf16[2,8,48,2880]{3,2,1,0:T(8,128)(2,1)S(1)}, bf16[2,8,48,2880]{3,2,1,0:T(8,128)(2,1)S(1)}) custom-call(bf16[8,4,2,128,768]{4,3,2,1,0:T(8,128)(2,1)S(1)} %copy-done, bf16[8,96,128]{2,1,0:T(8,128)(2,1)S(1)} %get-tuple-element.16.refs_1_, f32[1,2880]{1,0:T(1,128)S(1)} %broadcast_in_dim.60.refs_2_), custom_call_target="tpu_custom_call" | custom-call | tf_op jit(solution)/shard_map/fill_slots/pallas_call | solution.py:179
  104.8 2.7 fusion.38
  107.5 1.6 slice-done.1
  109.1 2.5 fusion.41
  111.7 2.3 fusion.17
  114.0 6.1 %convolution_convert_fusion.2 = bf16[384,2880]{0,1:T(8,128)(2,1)} fusion(bf16[2880,720]{0,1:T(8,128)(2,1)} %bitcast.109, bf16[384,360]{0,1:T(8,128)(2,1)S(1)} %get-tuple-element.43, bf16[384,360]{0,1:T(8,128)(2,1)S(1)} %get-tuple-element.44), kind=kOutput, calls=%fused_computation.10 | convolution fusion | flops 1594736640 | bytes 6912000 | tf_op jit(solution)/shard_map/dot_general | solution.py:35
  120.1 3.1 %copy.110 = bf16[384,2880]{1,0:T(8,128)(2,1)S(1)} copy(bf16[384,2880]{0,1:T(8,128)(2,1)} %convolution_convert_fusion.2) | data formatting | bytes 4423680 | tf_op jit(solution)/shard_map/convert_element_type | solution.py:309
  123.5 5.5 %fusion.40 = f32[384,720]{0,1:T(8,128)S(1)} fusion(bf16[384,2880]{1,0:T(8,128)(2,1)} %bitcast.117, bf16[2880,720]{0,1:T(8,128)(2,1)} %bitcast.107), kind=kOutput, calls=%fused_computation.99 | convolution fusion | flops 1592524800 | bytes 7464960 | tf_op jit(solution)/shard_map/dot_general | solution.py:13
  129.0 4.0 %fusion.15 = (f32[384]{0:T(512)S(1)}, bf16[384,360]{0,1:T(8,128)(2,1)}, bf16[384,360]{0,1:T(8,128)(2,1)S(1)}, bf16[384,360]{0,1:T(8,128)(2,1)}) fusion(f32[384,720]{0,1:T(8,128)S(1)} %fusion.40, f32[384]{0:T(512)S(1)} %reshape.227, bf16[384,2880]{1,0:T(8,128)(2,1)S(1)} %bitcast.119, bf16[2,360,2880]{2,1,0:T(8,128)(2,1)} %param.13), kind=kOutput, calls=%fused_computation.37 | convolution fusion | flops 799165056 | bytes 6269952 | tf_op jit(solution)/shard_map/dot_general | solution.py:19
  133.1 6.2 %convolution_convert_fusion.3 = bf16[384,2880]{0,1:T(8,128)(2,1)} fusion(bf16[2880,720]{0,1:T(8,128)(2,1)} %bitcast.108, bf16[384,360]{0,1:T(8,128)(2,1)S(1)} %get-tuple-element.41, bf16[384,360]{0,1:T(8,128)(2,1)} %get-tuple-element.42), kind=kOutput, calls=%fused_computation.11 | convolution fusion | flops 1594736640 | bytes 6912000 | tf_op jit(solution)/shard_map/dot_general | solution.py:35
  139.3 4.2 %copy.107 = bf16[384,2880]{1,0:T(8,128)(2,1)} copy(bf16[384,2880]{0,1:T(8,128)(2,1)} %convolution_convert_fusion.3) | data formatting | bytes 4423680 | tf_op jit(solution)/shard_map/convert_element_type | solution.py:309
  143.8 2.9 %concatenate.31 = bf16[8,48,2882]{2,1,0:T(8,128)(2,1)} concatenate(bf16[8,48,2880]{2,1,0:T(8,128)(2,1)S(1)} %bitcast.105, bf16[8,48,1]{2,1,0:T(8,128)(2,1)S(1)} %copy.111, bf16[8,48,1]{2,1,0:T(8,128)(2,1)S(1)} %copy.112), dimensions={2} | concatenate | bytes 4426752 | tf_op jit(solution)/shard_map/concatenate | solution.py:314
  146.7 4.7 %concatenate.29 = bf16[8,48,2882]{2,1,0:T(8,128)(2,1)} concatenate(bf16[8,48,2880]{2,1,0:T(8,128)(2,1)} %bitcast.106, bf16[8,48,1]{2,1,0:T(8,128)(2,1)S(1)} %copy.108, bf16[8,48,1]{2,1,0:T(8,128)(2,1)S(1)} %copy.109), dimensions={2} | concatenate | bytes 4426752 | tf_op jit(solution)/shard_map/concatenate | solution.py:314
  151.5 4.1 %pad_maximum_fusion.1 = bf16[8,96,2882]{2,1,0:T(8,128)(2,1)} fusion(bf16[8,48,2882]{2,1,0:T(8,128)(2,1)S(1)} %copy-done.1, bf16[8,48,2882]{2,1,0:T(8,128)(2,1)} %concatenate.29), kind=kLoop, calls=%fused_computation.6 | loop fusion | flops 8853504 | bytes 8853504 | tf_op jit(solution)/shard_map/concatenate | solution.py:313
  155.6 4.7 %all-to-all-start = ((bf16[8,96,2882]{2,1,0:T(8,128)(2,1)}), bf16[8,96,2882]{2,1,0:T(8,128)(2,1)}, u32[]{:S(2)}, u32[]{:S(2)}) async-start(bf16[8,96,2882]{2,1,0:T(8,128)(2,1)} %pad_maximum_fusion.1), calls=%async_computation | async-start | bytes 9043968 | tf_op jit(solution)/shard_map/all_to_all | solution.py:316
  160.5 1.7 dynamic-slice_bitcast_fusion
  162.6 2.7 fusion.5
  165.3 2.7 %fusion.4 = bf16[1,360,2880]{2,1,0:T(8,128)(2,1)} fusion(bf16[384,2880]{1,0:T(8,128)(2,1)S(1)} %bitcast.120, bf16[384,360]{0,1:T(8,128)(2,1)S(1)} %copy-done.15, f32[384]{0:T(512)S(1)} %reshape.227), kind=kOutput, calls=%fused_computation.14 | convolution fusion | flops 797713920 | bytes 4563456 | tf_op jit(solution)/shard_map/dot_general | solution.py:29
  168.0 4.4 %fusion.2 = bf16[1,2880,2,360]{1,3,2,0:T(8,128)(2,1)} fusion(bf16[384,2880,1]{1,0,2:T(8,128)(2,1)S(1)} %bitcast.118, bf16[2,360,384]{2,1,0:T(8,128)(2,1)S(1)} %bitcast.125), kind=kOutput, calls=%fused_computation.7 | convolution fusion | flops 1594598400 | bytes 6912000 | tf_op jit(solution)/shard_map/dot_general | solution.py:32
  172.3 40.6 %all-to-all-done = bf16[8,96,2882]{2,1,0:T(8,128)(2,1)} async-done(((bf16[8,96,2882]{2,1,0:T(8,128)(2,1)}), bf16[8,96,2882]{2,1,0:T(8,128)(2,1)}, u32[]{:S(2)}, u32[]{:S(2)}) %all-to-all-start) | async-done | bytes 4426784 | tf_op jit(solution)/shard_map/all_to_all | solution.py:316
  214.8 5.0 %fusion.6 = bf16[128,2880]{0,1:T(8,128)(2,1)} fusion(bf16[768,2882]{1,0:T(8,128)(2,1)} %bitcast.23, bf16[128,768]{1,0:T(8,128)(2,1)S(1)} %get-tuple-element.20), kind=kOutput, calls=%fused_computation.16 | convolution fusion | flops 566599680 | bytes 5360640 | tf_op jit(solution)/shard_map/dot_general | solution.py:324
  219.9 6.2 %fusion.3 = bf16[1,2880,2,360]{1,3,2,0:T(8,128)(2,1)} fusion(bf16[384,2880,1]{1,0,2:T(8,128)(2,1)} %bitcast.116, bf16[2,360,384]{2,1,0:T(8,128)(2,1)S(1)} %bitcast.126), kind=kOutput, calls=%fused_computation.8 | convolution fusion | flops 1594598400 | bytes 6912000 | tf_op jit(solution)/shard_map/dot_general | solution.py:32
  226.1 2.5 pad_maximum_fusion.2
  228.6 6.6 %pad_maximum_fusion = bf16[2,2880,2,360]{1,3,2,0:T(8,128)(2,1)} fusion(bf16[1,2880,2,360]{1,3,2,0:T(8,128)(2,1)} %fusion.3, bf16[1,2880,2,360]{1,3,2,0:T(8,128)(2,1)S(1)} %bitcast.114), kind=kLoop, calls=%fused_computation | loop fusion | flops 4147200 | bytes 16588800 | tf_op jit(solution)/shard_map/stack | solution.py:363
  235.1 14.1 %reduce-scatter.2.cloned.1.call-done = bf16[128,720]{0,1:T(8,128)(2,1)} async-done(((bf16[128,2880]{0,1:T(8,128)(2,1)}), bf16[128,720]{0,1:T(8,128)(2,1)}) %reduce-scatter.2.cloned.1.call-update) | async-done | bytes 184336 | tf_op jit(solution)/shard_map/reduce_scatter | solution.py:334
  251.7 7.0 %exchange.1 = (f32[4,8,128]{2,1,0:T(8,128)}, f32[8,8,128]{2,1,0:T(8,128)}) custom-call(f32[8,128]{1,0:T(8,128)} %pad_bitcast_fusion.1.refs_0_, f32[8,128]{1,0:T(8,128)} %pad_bitcast_fusion.refs_1_), custom_call_target="tpu_custom_call" | custom-call | tf_op jit(solution)/shard_map/exchange/pallas_call | solution.py:231
  261.4 1.8 fusion.28
  (101 shorter events, 19.6 us)
Async XLA Ops:
  93.4 4.6 %copy-start = (bf16[8,4,2,128,768]{4,3,2,1,0:T(8,128)(2,1)S(1)}, bf16[8,4,2,128,768]{4,3,2,1,0:T(8,128)(2,1)}, u32[]{:S(2)}) copy-start(bf16[8,4,2,128,768]{4,3,2,1,0:T(8,128)(2,1)} %spread.1.refs_0_) | copy-start | bytes 37748740
  98.0 9.5 %slice-start = ((s8[4239360]{0:T(1024)(128)(4,1)}), s8[45056]{0:T(1024)(128)(4,1)S(1)}, s32[]{:S(2)}) async-start(s8[4239360]{0:T(1024)(128)(4,1)} %bitcast.110), calls=%async_computation.3 | async-start | bytes 90112
  104.8 4.3 %slice-start.1 = ((s8[4239360]{0:T(1024)(128)(4,1)}), s8[4194304]{0:T(1024)(128)(4,1)S(1)}, s32[]{:S(2)}) async-start(s8[4239360]{0:T(1024)(128)(4,1)} %bitcast.110), calls=%async_computation.4 | async-start | bytes 8388608
  104.8 6.8 %slice-start.4 = ((s8[4239360]{0:T(1024)(128)(4,1)}), s8[4194304]{0:T(1024)(128)(4,1)S(1)}, s32[]{:S(2)}) async-start(s8[4239360]{0:T(1024)(128)(4,1)} %bitcast.130), calls=%async_computation.7 | async-start | bytes 8388608
  107.5 4.1 %copy-start.2 = (bf16[1,8,48,2880]{3,2,1,0:T(8,128)(2,1)}, bf16[1,8,48,2880]{3,2,1,0:T(8,128)(2,1)S(1)}, u32[]{:S(2)}) copy-start(bf16[1,8,48,2880]{3,2,1,0:T(8,128)(2,1)S(1)} %get-tuple-element.34) | copy-start | bytes 6635524
  107.5 4.1 %copy-start.6 = (bf16[1,8,48,2880]{3,2,1,0:T(8,128)(2,1)}, bf16[1,8,48,2880]{3,2,1,0:T(8,128)(2,1)S(1)}, u32[]{:S(2)}) copy-start(bf16[1,8,48,2880]{3,2,1,0:T(8,128)(2,1)S(1)} %get-tuple-element.49) | copy-start | bytes 6635524
  109.1 2.5 slice-start.5
  123.5 5.5 %copy-start.4 = (bf16[1,8,48,2880]{3,2,1,0:T(8,128)(2,1)S(1)}, bf16[1,8,48,2880]{3,2,1,0:T(8,128)(2,1)}, u32[]{:S(2)}) copy-start(bf16[1,8,48,2880]{3,2,1,0:T(8,128)(2,1)} %get-tuple-element.50) | copy-start | bytes 6635524
  146.7 4.8 %copy-start.1 = (bf16[8,48,2882]{2,1,0:T(8,128)(2,1)S(1)}, bf16[8,48,2882]{2,1,0:T(8,128)(2,1)}, u32[]{:S(2)}) copy-start(bf16[8,48,2882]{2,1,0:T(8,128)(2,1)} %concatenate.31) | copy-start | bytes 6640132
  155.6 4.8 %copy-start.13 = (bf16[2880]{0:T(1024)(128)(2,1)S(1)}, bf16[2880]{0:T(1024)(128)(2,1)}, u32[]{:S(2)}) copy-start(bf16[2880]{0:T(1024)(128)(2,1)} %param.9) | copy-start | bytes 17284
  155.6 4.9 %copy-start.12 = (bf16[384,360]{0,1:T(8,128)(2,1)S(1)}, bf16[384,360]{0,1:T(8,128)(2,1)}, u32[]{:S(2)}) copy-start(bf16[384,360]{0,1:T(8,128)(2,1)} %get-tuple-element.42) | copy-start | bytes 829444
  155.6 57.4 %all-to-all-start = ((bf16[8,96,2882]{2,1,0:T(8,128)(2,1)}), bf16[8,96,2882]{2,1,0:T(8,128)(2,1)}, u32[]{:S(2)}, u32[]{:S(2)}) async-start(bf16[8,96,2882]{2,1,0:T(8,128)(2,1)} %pad_maximum_fusion.1), calls=%async_computation | async-start | bytes 9043968 | tf_op jit(solution)/shard_map/all_to_all | solution.py:316
  160.3 88.9 %reduce-scatter.2.cloned.1.call-start = ((), (), s32[]{:S(2)}) async-start(), calls=%async_computation.2 | async-start | bytes 921600 | tf_op jit(solution)/shard_map/reduce_scatter | solution.py:334
  160.5 2.1 copy-start.7
  160.5 2.1 copy-start.14
  162.6 2.7 copy-start.5
  162.6 2.7 copy-start.15
  165.3 2.7 %copy-start.3 = (bf16[1,8,48,2880]{3,2,1,0:T(8,128)(2,1)S(1)}, bf16[1,8,48,2880]{3,2,1,0:T(8,128)(2,1)}, u32[]{:S(2)}) copy-start(bf16[1,8,48,2880]{3,2,1,0:T(8,128)(2,1)} %get-tuple-element.33) | copy-start | bytes 6635524
  219.8 6.3 %copy-start.9 = (bf16[1,360,2880]{2,1,0:T(8,128)(2,1)S(1)}, bf16[1,360,2880]{2,1,0:T(8,128)(2,1)}, u32[]{:S(2)}) copy-start(bf16[1,360,2880]{2,1,0:T(8,128)(2,1)} %fusion.4) | copy-start | bytes 6220804
  219.9 6.2 %copy-start.8 = (bf16[1,360,2880]{2,1,0:T(8,128)(2,1)S(1)}, bf16[1,360,2880]{2,1,0:T(8,128)(2,1)}, u32[]{:S(2)}) copy-start(bf16[1,360,2880]{2,1,0:T(8,128)(2,1)} %fusion.5) | copy-start | bytes 6220804
  219.9 8.7 %slice-start.2 = ((s8[4239360]{0:T(1024)(128)(4,1)}), s8[4194304]{0:T(1024)(128)(4,1)S(1)}, s32[]{:S(2)}) async-start(s8[4239360]{0:T(1024)(128)(4,1)} %bitcast.113), calls=%async_computation.5 | async-start | bytes 8388608
  226.1 2.5 slice-start.3
  228.6 20.7 %copy-start.10 = (bf16[128,720]{0,1:T(8,128)(2,1)S(1)}, bf16[128,720]{0,1:T(8,128)(2,1)}, u32[]{:S(2)}) copy-start(bf16[128,720]{0,1:T(8,128)(2,1)} %param.7) | copy-start | bytes 552964
  228.6 32.8 %copy-start.11 = (bf16[128,720]{0,1:T(8,128)(2,1)S(1)}, bf16[128,720]{0,1:T(8,128)(2,1)}, u32[]{:S(2)}) copy-start(bf16[128,720]{0,1:T(8,128)(2,1)} %param.8) | copy-start | bytes 552964
Sparse Core Ops, SparseCore 0:
  219.9 29.3 reduce-scatter.1

commit v2 on v1

--- a/solution.py
+++ b/solution.py
@@ -246,6 +246,47 @@
     )(stat, gain)
 
 
+def scatter_kernel(depth, pieces_ref, out_ref, sends, lands, keep):
+    z = lax.axis_index("dp")
+    barrier = pltpu.get_barrier_semaphore()
+    for k in range(1, depth):
+        pl.semaphore_signal(barrier, inc=1, device_id={"dp": (z + k) % depth})
+    pl.semaphore_wait(barrier, depth - 1)
+    running = []
+    for k in range(1, depth):
+        copy = pltpu.make_async_remote_copy(
+            src_ref=pieces_ref.at[(z + k) % depth],
+            dst_ref=out_ref.at[k],
+            send_sem=sends.at[k],
+            recv_sem=lands.at[k],
+            device_id={"dp": (z + k) % depth},
+        )
+        copy.start()
+        running.append(copy)
+    copy = pltpu.make_async_copy(pieces_ref.at[z], out_ref.at[0], keep)
+    copy.start()
+    running.append(copy)
+    for copy in running:
+        copy.wait()
+
+
+def scatter(pieces):
+    depth = pieces.shape[0]
+    return pl.pallas_call(
+        lambda *refs: scatter_kernel(depth, *refs),
+        out_shape=jax.ShapeDtypeStruct(pieces.shape, pieces.dtype),
+        in_specs=[pl.BlockSpec(memory_space=pltpu.VMEM)],
+        out_specs=pl.BlockSpec(memory_space=pltpu.VMEM),
+        scratch_shapes=[
+            pltpu.SemaphoreType.DMA((depth,)),
+            pltpu.SemaphoreType.DMA((depth,)),
+            pltpu.SemaphoreType.DMA,
+        ],
+        compiler_params=pltpu.CompilerParams(collective_id=2, has_side_effects=True),
+        name="scatter",
+    )(pieces)
+
+
 def plane_body(tokens, upstream, norm_gain, experts, route_weights, w_gate_up, w_down):
     dp_count = lax.axis_size("dp")
     seq_count = lax.axis_size("seq")
@@ -331,9 +372,8 @@
         ),
         axis=2,
     )
-    dnormed = lax.psum_scatter(
-        combined.astype(jnp.bfloat16), "dp", scatter_dimension=1, tiled=True
-    ).astype(jnp.float32)
+    pieces = jnp.stack(jnp.split(combined.astype(jnp.bfloat16), dp_count, axis=1))
+    dnormed = jnp.sum(scatter(pieces).astype(jnp.float32), axis=0)
     my_gain = lax.dynamic_slice_in_dim(gain, lax.axis_index("dp") * part, part, 0)
     xhat = tokens.astype(jnp.float32) * my_inv
     u = dnormed * my_gain[None, :]

time: 271 us -> 258 us (0.952)
  Pallas kernels: 79.2 us -> 109 us
  waiting for transfers between devices: 54.7 us -> 31.3 us
  between operations: 14.4 us -> 1.01 us
  matrix products: 47.4 us -> 39.2 us
    pallas_call x0 -> x1, Pallas kernels: none -> 23.2 us  [scatter(): pl.pallas_call(lambda *refs: scatter_kernel(depth, *refs), out_shape=jax....]
    reduce_scatter x1 -> x0, waiting for transfers between devices: 14.1 us -> none  [plane_body(): lax.psum_scatter(combined.astype(jnp.bfloat16), 'dp', scatter_dimension=1...]
    all_to_all x1, waiting for transfers between devices: 40.6 us -> 31.3 us  [plane_body(): lax.all_to_all(leaving, 'seq', split_axis=0, concat_axis=0, tiled=True)]
    pallas_call x1, Pallas kernels: 7.04 us -> 13.6 us  [exchange(): pl.pallas_call(lambda *refs: exchange_kernel(depth, peers, *refs), out_sh...]
    dot_general x2, matrix products: 10.6 us -> 6.78 us  [expert_terms(): lax.dot_general(x_rows, dproj, (((0,), (0,)), ((), ())), preferred_elemen...]
    unnamed x48 -> x45, local copies, waits for them, and re-layouts: 10.1 us -> 12.1 us
  transfers between devices with their start and end apart: 2 -> 1, of which waited for: 2 -> 1; matrix products, arithmetic and copies ran while one was open for 10% -> 8% of each run, Pallas kernels for 0% -> 0%
where the time goes in v2:
time: 258 us; the launch traced here: 257 us
  Pallas kernels  109 us (42%)
  local copies, waits for them, and re-layouts  44 us (17%)
  matrix products  39.2 us (15%)
  waiting for transfers between devices  31.3 us (12%)
  other arithmetic  27.3 us (11%)
  starting transfers between devices  4.73 us (2%)
    pallas_call x1, Pallas kernels, spread(): pl.pallas_call(lambda *refs: spread_kernel(depth, *refs), out_shape=jax.S...  65.4 us
    all_to_all x1, waiting for transfers between devices, plane_body(): lax.all_to_all(leaving, 'seq', split_axis=0, concat_axis=0, tiled=True)  31.3 us
    pallas_call x1, Pallas kernels, scatter(): pl.pallas_call(lambda *refs: scatter_kernel(depth, *refs), out_shape=jax....  23.2 us
    pallas_call x1, Pallas kernels, exchange(): pl.pallas_call(lambda *refs: exchange_kernel(depth, peers, *refs), out_sh...  13.6 us
    dot_general x2, matrix products, expert_terms(): lax.dot_general(dproj, flat_gu, (((1,), (1,)), ((), ())), preferred_eleme...  12.4 us
    unnamed x45, local copies, waits for them, and re-layouts  12.1 us
    dot_general x2, matrix products, expert_terms(): projected = jnp.dot(x_rows, flat_gu, preferred_element_type=jnp.float32)  7.95 us
    concatenate x2, local copies, waits for them, and re-layouts, plane_body(): jnp.concatenate(t, axis=2)  7.7 us
  transfers between devices with their start and end apart: 1, of which 1 were waited for; matrix products, arithmetic and copies ran while one was open for 8% of the time, Pallas kernels for 0%

profile of v2, /device:TPU:0, one launch (start us, length us, event | category | flops | bytes accessed | tf_op | source)
XLA Modules:
  0.0 256.6 jit_solution(6420860545433163216)
XLA Ops:
  6.8 5.9 %fusion.30 = (bf16[1,2880,2,360]{1,3,2,0:T(8,128)(2,1)}, bf16[1,2880,2,360]{1,3,2,0:T(8,128)(2,1)}) fusion(bf16[2,2880,2,360]{1,3,2,0:T(8,128)(2,1)} %param.12), kind=kLoop, calls=%fused_computation.96 | loop fusion | bytes 16588800 | tf_op jit(solution)/shard_map/slice | solution.py:346
  13.6 65.4 %spread.1.refs_0_ = bf16[8,4,2,128,768]{4,3,2,1,0:T(8,128)(2,1)} custom-call(bf16[2,128,768]{2,1,0:T(8,128)(2,1)} %pad_maximum_fusion.6.refs_0_), custom_call_target="tpu_custom_call" | custom-call | tf_op jit(solution)/shard_map/spread/pallas_call | solution.py:138
  79.0 1.4 slice_convert_fusion
  81.6 2.3 convert_reduce_fusion
  86.9 4.6 %copy-done = bf16[8,4,2,128,768]{4,3,2,1,0:T(8,128)(2,1)S(1)} copy-done((bf16[8,4,2,128,768]{4,3,2,1,0:T(8,128)(2,1)S(1)}, bf16[8,4,2,128,768]{4,3,2,1,0:T(8,128)(2,1)}, u32[]{:S(2)}) %copy-start) | copy-done | bytes 12582936
  91.5 6.8 %fill_slots.1 = (bf16[2,8,48,2880]{3,2,1,0:T(8,128)(2,1)S(1)}, bf16[2,8,48,2880]{3,2,1,0:T(8,128)(2,1)S(1)}) custom-call(bf16[8,4,2,128,768]{4,3,2,1,0:T(8,128)(2,1)S(1)} %copy-done, bf16[8,96,128]{2,1,0:T(8,128)(2,1)S(1)} %get-tuple-element.31.refs_1_, f32[1,2880]{1,0:T(1,128)S(1)} %broadcast_in_dim.60.refs_2_), custom_call_target="tpu_custom_call" | custom-call | tf_op jit(solution)/shard_map/fill_slots/pallas_call | solution.py:179
  98.3 2.7 %fusion.31 = (bf16[1,8,48,2880]{3,2,1,0:T(8,128)(2,1)}, bf16[1,8,48,2880]{3,2,1,0:T(8,128)(2,1)S(1)}, bf16[1,8,48,2880]{3,2,1,0:T(8,128)(2,1)S(1)}, bf16[1,8,48,2880]{3,2,1,0:T(8,128)(2,1)}) fusion(bf16[2,8,48,2880]{3,2,1,0:T(8,128)(2,1)S(1)} %get-tuple-element.10, bf16[2,8,48,2880]{3,2,1,0:T(8,128)(2,1)S(1)} %get-tuple-element.9), kind=kLoop, calls=%fused_computation.97 | loop fusion | bytes 17694720 | tf_op jit(solution)/shard_map/slice | solution.py:346
  101.0 1.6 slice-done.1
  102.6 2.5 fusion.34
  105.1 2.2 fusion.17
  108.1 6.1 %convolution_convert_fusion.2 = bf16[384,2880]{0,1:T(8,128)(2,1)} fusion(bf16[2880,720]{0,1:T(8,128)(2,1)} %bitcast.117, bf16[384,360]{0,1:T(8,128)(2,1)S(1)} %get-tuple-element.58, bf16[384,360]{0,1:T(8,128)(2,1)S(1)} %get-tuple-element.59), kind=kOutput, calls=%fused_computation.10 | convolution fusion | flops 1594736640 | bytes 6912000 | tf_op jit(solution)/shard_map/dot_general | solution.py:35
  114.2 3.1 %copy.145 = bf16[384,2880]{1,0:T(8,128)(2,1)S(1)} copy(bf16[384,2880]{0,1:T(8,128)(2,1)} %convolution_convert_fusion.2) | data formatting | bytes 4423680 | tf_op jit(solution)/shard_map/convert_element_type | solution.py:350
  117.6 5.5 %fusion.33 = f32[384,720]{0,1:T(8,128)S(1)} fusion(bf16[384,2880]{1,0:T(8,128)(2,1)} %bitcast.123, bf16[2880,720]{0,1:T(8,128)(2,1)} %bitcast.115), kind=kOutput, calls=%fused_computation.99 | convolution fusion | flops 1592524800 | bytes 7464960 | tf_op jit(solution)/shard_map/dot_general | solution.py:13
  123.1 4.1 %fusion.15 = (f32[384]{0:T(512)S(1)}, bf16[384,360]{0,1:T(8,128)(2,1)}, bf16[384,360]{0,1:T(8,128)(2,1)}, bf16[384,360]{0,1:T(8,128)(2,1)}) fusion(f32[384,720]{0,1:T(8,128)S(1)} %fusion.33, f32[384]{0:T(512)S(1)} %reshape.227, bf16[384,2880]{1,0:T(8,128)(2,1)S(1)} %bitcast.125, bf16[2,360,2880]{2,1,0:T(8,128)(2,1)} %param.13), kind=kOutput, calls=%fused_computation.39 | convolution fusion | flops 799165056 | bytes 6269952 | tf_op jit(solution)/shard_map/dot_general | solution.py:19
  127.3 6.3 %convolution_convert_fusion.3 = bf16[384,2880]{0,1:T(8,128)(2,1)} fusion(bf16[2880,720]{0,1:T(8,128)(2,1)} %bitcast.116, bf16[384,360]{0,1:T(8,128)(2,1)} %get-tuple-element.56, bf16[384,360]{0,1:T(8,128)(2,1)} %get-tuple-element.57), kind=kOutput, calls=%fused_computation.11 | convolution fusion | flops 1594736640 | bytes 6912000 | tf_op jit(solution)/shard_map/dot_general | solution.py:35
  133.6 4.2 %copy.142 = bf16[384,2880]{1,0:T(8,128)(2,1)} copy(bf16[384,2880]{0,1:T(8,128)(2,1)} %convolution_convert_fusion.3) | data formatting | bytes 4423680 | tf_op jit(solution)/shard_map/convert_element_type | solution.py:350
  138.0 2.9 %concatenate.31 = bf16[8,48,2882]{2,1,0:T(8,128)(2,1)} concatenate(bf16[8,48,2880]{2,1,0:T(8,128)(2,1)S(1)} %bitcast.113, bf16[8,48,1]{2,1,0:T(8,128)(2,1)S(1)} %copy.146, bf16[8,48,1]{2,1,0:T(8,128)(2,1)S(1)} %copy.147), dimensions={2} | concatenate | bytes 4426752 | tf_op jit(solution)/shard_map/concatenate | solution.py:355
  141.0 4.8 %concatenate.29 = bf16[8,48,2882]{2,1,0:T(8,128)(2,1)} concatenate(bf16[8,48,2880]{2,1,0:T(8,128)(2,1)} %bitcast.114, bf16[8,48,1]{2,1,0:T(8,128)(2,1)S(1)} %copy.143, bf16[8,48,1]{2,1,0:T(8,128)(2,1)S(1)} %copy.144), dimensions={2} | concatenate | bytes 4426752 | tf_op jit(solution)/shard_map/concatenate | solution.py:355
  145.8 4.0 %pad_maximum_fusion.1 = bf16[8,96,2882]{2,1,0:T(8,128)(2,1)} fusion(bf16[8,48,2882]{2,1,0:T(8,128)(2,1)S(1)} %copy-done.1, bf16[8,48,2882]{2,1,0:T(8,128)(2,1)} %concatenate.29), kind=kLoop, calls=%fused_computation.6 | loop fusion | flops 8853504 | bytes 8853504 | tf_op jit(solution)/shard_map/concatenate | solution.py:354
  149.8 4.7 %all-to-all-start = ((bf16[8,96,2882]{2,1,0:T(8,128)(2,1)}), bf16[8,96,2882]{2,1,0:T(8,128)(2,1)}, u32[]{:S(2)}, u32[]{:S(2)}) async-start(bf16[8,96,2882]{2,1,0:T(8,128)(2,1)} %pad_maximum_fusion.1), calls=%async_computation | async-start | bytes 9043968 | tf_op jit(solution)/shard_map/all_to_all | solution.py:357
  154.8 1.7 dynamic-slice_bitcast_fusion
  156.8 1.3 fusion.5
  158.4 1.3 fusion.4
  160.1 2.4 fusion.2
  162.5 4.4 %fusion.3 = bf16[1,2880,2,360]{1,3,2,0:T(8,128)(2,1)} fusion(bf16[384,2880,1]{1,0,2:T(8,128)(2,1)S(1)} %bitcast.122, bf16[2,360,384]{2,1,0:T(8,128)(2,1)S(1)} %bitcast.131), kind=kOutput, calls=%fused_computation.8 | convolution fusion | flops 1594598400 | bytes 6912000 | tf_op jit(solution)/shard_map/dot_general | solution.py:32
  166.9 2.5 pad_maximum_fusion.2
  169.3 6.5 %pad_maximum_fusion = bf16[2,2880,2,360]{1,3,2,0:T(8,128)(2,1)} fusion(bf16[1,2880,2,360]{1,3,2,0:T(8,128)(2,1)} %fusion.3, bf16[1,2880,2,360]{1,3,2,0:T(8,128)(2,1)S(1)} %fusion.2), kind=kLoop, calls=%fused_computation | loop fusion | flops 4147200 | bytes 16588800 | tf_op jit(solution)/shard_map/stack | solution.py:403
  175.9 31.3 %all-to-all-done = bf16[8,96,2882]{2,1,0:T(8,128)(2,1)} async-done(((bf16[8,96,2882]{2,1,0:T(8,128)(2,1)}), bf16[8,96,2882]{2,1,0:T(8,128)(2,1)}, u32[]{:S(2)}, u32[]{:S(2)}) %all-to-all-start) | async-done | bytes 4426784 | tf_op jit(solution)/shard_map/all_to_all | solution.py:357
  208.9 3.1 %fusion.6 = bf16[128,2880]{1,0:T(8,128)(2,1)S(1)} fusion(bf16[768,2882]{1,0:T(8,128)(2,1)} %bitcast.23, bf16[128,768]{1,0:T(8,128)(2,1)S(1)} %get-tuple-element.35), kind=kOutput, calls=%fused_computation.16 | convolution fusion | flops 566599680 | bytes 5360640 | tf_op jit(solution)/shard_map/dot_general | solution.py:365
  213.3 23.2 %scatter.1 = bf16[4,128,720]{2,1,0:T(8,128)(2,1)} custom-call(bf16[4,128,720]{2,1,0:T(8,128)(2,1)} %pad_maximum_fusion.3.refs_0_), custom_call_target="tpu_custom_call" | custom-call | tf_op jit(solution)/shard_map/scatter/pallas_call | solution.py:275
  239.3 13.6 %exchange.1 = (f32[4,8,128]{2,1,0:T(8,128)}, f32[8,8,128]{2,1,0:T(8,128)}) custom-call(f32[8,128]{1,0:T(8,128)} %pad_bitcast_fusion.1.refs_0_, f32[8,128]{1,0:T(8,128)} %pad_bitcast_fusion.refs_1_), custom_call_target="tpu_custom_call" | custom-call | tf_op jit(solution)/shard_map/exchange/pallas_call | solution.py:231
  254.2 1.4 reduce_sum.145
  (98 shorter events, 21.9 us)
Async XLA Ops:
  86.9 4.6 %copy-start = (bf16[8,4,2,128,768]{4,3,2,1,0:T(8,128)(2,1)S(1)}, bf16[8,4,2,128,768]{4,3,2,1,0:T(8,128)(2,1)}, u32[]{:S(2)}) copy-start(bf16[8,4,2,128,768]{4,3,2,1,0:T(8,128)(2,1)} %spread.1.refs_0_) | copy-start | bytes 37748740
  91.5 9.5 %slice-start = ((s8[4239360]{0:T(1024)(128)(4,1)}), s8[45056]{0:T(1024)(128)(4,1)S(1)}, s32[]{:S(2)}) async-start(s8[4239360]{0:T(1024)(128)(4,1)} %bitcast.118), calls=%async_computation.1 | async-start | bytes 90112
  98.3 4.3 %slice-start.1 = ((s8[4239360]{0:T(1024)(128)(4,1)}), s8[4194304]{0:T(1024)(128)(4,1)S(1)}, s32[]{:S(2)}) async-start(s8[4239360]{0:T(1024)(128)(4,1)} %bitcast.118), calls=%async_computation.2 | async-start | bytes 8388608
  98.3 6.8 %slice-start.2 = ((s8[4239360]{0:T(1024)(128)(4,1)}), s8[4194304]{0:T(1024)(128)(4,1)S(1)}, s32[]{:S(2)}) async-start(s8[4239360]{0:T(1024)(128)(4,1)} %bitcast.136), calls=%async_computation.3 | async-start | bytes 8388608
  101.0 4.1 %copy-start.2 = (bf16[1,8,48,2880]{3,2,1,0:T(8,128)(2,1)}, bf16[1,8,48,2880]{3,2,1,0:T(8,128)(2,1)S(1)}, u32[]{:S(2)}) copy-start(bf16[1,8,48,2880]{3,2,1,0:T(8,128)(2,1)S(1)} %get-tuple-element.49) | copy-start | bytes 6635524
  101.0 4.1 %copy-start.7 = (bf16[1,8,48,2880]{3,2,1,0:T(8,128)(2,1)}, bf16[1,8,48,2880]{3,2,1,0:T(8,128)(2,1)S(1)}, u32[]{:S(2)}) copy-start(bf16[1,8,48,2880]{3,2,1,0:T(8,128)(2,1)S(1)} %get-tuple-element.68) | copy-start | bytes 6635524
  102.6 2.5 slice-start.3
  107.4 0.7 copy-start.9
  117.6 5.5 %copy-start.5 = (bf16[1,8,48,2880]{3,2,1,0:T(8,128)(2,1)S(1)}, bf16[1,8,48,2880]{3,2,1,0:T(8,128)(2,1)}, u32[]{:S(2)}) copy-start(bf16[1,8,48,2880]{3,2,1,0:T(8,128)(2,1)} %get-tuple-element.69) | copy-start | bytes 6635524
  141.0 4.8 %copy-start.1 = (bf16[8,48,2882]{2,1,0:T(8,128)(2,1)S(1)}, bf16[8,48,2882]{2,1,0:T(8,128)(2,1)}, u32[]{:S(2)}) copy-start(bf16[8,48,2882]{2,1,0:T(8,128)(2,1)} %concatenate.31) | copy-start | bytes 6640132
  149.7 4.8 %copy-start.13 = (bf16[2880]{0:T(1024)(128)(2,1)S(1)}, bf16[2880]{0:T(1024)(128)(2,1)}, u32[]{:S(2)}) copy-start(bf16[2880]{0:T(1024)(128)(2,1)} %param.9) | copy-start | bytes 17284
  149.7 4.9 %copy-start.10 = (bf16[384,360]{0,1:T(8,128)(2,1)S(1)}, bf16[384,360]{0,1:T(8,128)(2,1)}, u32[]{:S(2)}) copy-start(bf16[384,360]{0,1:T(8,128)(2,1)} %copy-done.9) | copy-start | bytes 829444
  149.7 4.9 %copy-start.11 = (bf16[384,360]{0,1:T(8,128)(2,1)S(1)}, bf16[384,360]{0,1:T(8,128)(2,1)}, u32[]{:S(2)}) copy-start(bf16[384,360]{0,1:T(8,128)(2,1)} %get-tuple-element.56) | copy-start | bytes 829444
  149.8 4.9 %copy-start.12 = (bf16[384,360]{0,1:T(8,128)(2,1)S(1)}, bf16[384,360]{0,1:T(8,128)(2,1)}, u32[]{:S(2)}) copy-start(bf16[384,360]{0,1:T(8,128)(2,1)} %get-tuple-element.57) | copy-start | bytes 829444
  149.8 57.4 %all-to-all-start = ((bf16[8,96,2882]{2,1,0:T(8,128)(2,1)}), bf16[8,96,2882]{2,1,0:T(8,128)(2,1)}, u32[]{:S(2)}, u32[]{:S(2)}) async-start(bf16[8,96,2882]{2,1,0:T(8,128)(2,1)} %pad_maximum_fusion.1), calls=%async_computation | async-start | bytes 9043968 | tf_op jit(solution)/shard_map/all_to_all | solution.py:357
  154.7 2.1 copy-start.8
  154.7 2.1 copy-start.14
  156.8 1.6 copy-start.6
  156.8 1.6 copy-start.15
  158.4 1.6 copy-start.4
  160.1 2.4 copy-start.3
